TPU v7x, 256 devices: a whole 4x4x8 slice. The times are simulated.
256 devices in a mesh: row: 32 (over z_lo, x, y), col: 8 (over z_hi, core).
Axes of the slice: x: 4, y: 4, z: 8 (z_hi: 4, z_lo: 2; z = z_hi * 2 + z_lo), core: 2. Of those that a mesh axis runs over, the one named last changes fastest.
Arguments:
- grad_out: bfloat16 [64, 512, 2048], P(None, 'row', 'col'), may hold values from -6 to 6
- row_feat: bfloat16 [512, 64], P('row'), may hold values from -6 to 6
- col_feat: bfloat16 [2048, 64], P('col'), may hold values from -6 to 6
- conv_one: bfloat16 [3, 3, 64, 64], replicated, may hold values from -0.25 to 0.25
- bias_one: float32 [64], replicated, may hold values from -3 to 3
- conv_two: bfloat16 [3, 3, 64, 64], replicated, may hold values from -0.25 to 0.25
Outputs:
- row_grad: float32 [512, 64], P('row')
- col_grad: float32 [2048, 64], P('col')
- grad_conv_one: float32 [3, 3, 64, 64], replicated
- grad_bias: float32 [64], replicated
- grad_conv_two: float32 [3, 3, 64, 64], replicated
All inputs are finite; a program needn't handle non-finite values.
Results may differ from a plain program's by a relative error of at most 0.0065.
Values may be sent and summed in bfloat16 or wider, within the bound.
No kernel may reach another device: no remote copies, remote signals or barrier semaphores. Data moves between devices by JAX's collectives and lax.ppermute only.
A program may use at most 128 MiB of HBM per device.

v0:
```python
import math
import jax
import jax.numpy as jnp
from jax import lax
from jax.sharding import PartitionSpec as P


def extended(block, sides, width):
    for axis, dim in sides:
        count = lax.axis_size(axis)
        forward = [(i, i + 1) for i in range(count - 1)]
        backward = [(target, source) for source, target in forward]
        low = lax.ppermute(
            lax.slice_in_dim(block, block.shape[dim] - width, None, axis=dim), axis, forward
        )
        high = lax.ppermute(lax.slice_in_dim(block, 0, width, axis=dim), axis, backward)
        block = jnp.concatenate([low, block, high], axis=dim)
    return block


def conv_valid(kernel, field):
    result = lax.conv_general_dilated(
        field[None],
        kernel,
        (1, 1),
        "VALID",
        rhs_dilation=(8, 8),
        dimension_numbers=("NCHW", "HWOI", "NCHW"),
        preferred_element_type=jnp.float32,
    )
    return result[0]


def flipped(kernel):
    return jnp.transpose(kernel[::-1, ::-1], (0, 1, 3, 2))


def tap_grads(upper, field, base_r, base_c, rows, cols):
    taps = []
    for tap_r in range(3):
        line = []
        for tap_c in range(3):
            top = base_r + 8 * (tap_r - 1)
            left = base_c + 8 * (tap_c - 1)
            piece = field[:, top : top + rows, left : left + cols]
            line.append(
                lax.dot_general(
                    upper, piece, (((1, 2), (1, 2)), ((), ())), preferred_element_type=jnp.float32
                )
            )
        taps.append(jnp.stack(line))
    return jnp.stack(taps)


def slope(pre):
    sig = jax.nn.sigmoid(pre)
    return sig * (1.0 + pre * (1.0 - sig))


def inside_mask(row_first, col_first, margin, tile_rows, tile_cols, total_rows, total_cols):
    global_rows = row_first + jnp.arange(tile_rows + 2 * margin, dtype=jnp.int32) - margin
    global_cols = col_first + jnp.arange(tile_cols + 2 * margin, dtype=jnp.int32) - margin
    return ((global_rows >= 0) & (global_rows < total_rows))[:, None] & (
        (global_cols >= 0) & (global_cols < total_cols)
    )[None, :]


def shards(grad_out, row_feat, col_feat, conv_one, bias_one, conv_two):
    chans, tile_rows, tile_cols = grad_out.shape
    total_rows = tile_rows * lax.axis_size("row")
    total_cols = tile_cols * lax.axis_size("col")
    row_first = lax.axis_index("row") * tile_rows
    col_first = lax.axis_index("col") * tile_cols
    row_ext = extended(row_feat, (("row", 0),), 16)
    col_ext = extended(col_feat, (("col", 0),), 16)
    outer = inside_mask(row_first, col_first, 16, tile_rows, tile_cols, total_rows, total_cols)
    summed = row_ext.T.astype(jnp.float32)[:, :, None] + col_ext.T.astype(jnp.float32)[:, None, :]
    field = jnp.where(outer[None], summed, 0.0).astype(jnp.bfloat16)
    pre = conv_valid(conv_one, field) + bias_one[:, None, None]
    inside = inside_mask(row_first, col_first, 8, tile_rows, tile_cols, total_rows, total_cols)
    act = jnp.where(inside[None], jax.nn.silu(pre), 0.0).astype(jnp.bfloat16)
    grad_ext = extended(grad_out, (("row", 1), ("col", 2)), 16)
    back = conv_valid(flipped(conv_two), grad_ext)
    inner = jnp.where(inside[None], back * slope(pre), 0.0).astype(jnp.bfloat16)
    spread = conv_valid(flipped(conv_one), inner)
    inner_tile = inner[:, 8 : 8 + tile_rows, 8 : 8 + tile_cols]
    grad_in = grad_out.astype(jnp.float32) + spread
    row_part = jnp.sum(grad_in, axis=2).T
    col_part = jnp.sum(grad_in, axis=1).T
    grad_one = tap_grads(inner_tile, field, 16, 16, tile_rows, tile_cols)
    grad_two = tap_grads(grad_out, act, 8, 8, tile_rows, tile_cols)
    bias_part = jnp.sum(inner_tile.astype(jnp.float32), axis=(1, 2))
    row_grad = lax.psum(row_part, "col") / math.sqrt(total_cols)
    col_grad = lax.psum(col_part, "row") / math.sqrt(total_rows)
    sum_one, sum_bias, sum_two = lax.psum((grad_one, bias_part, grad_two), ("row", "col"))
    whole = math.sqrt(total_rows * total_cols)
    return (row_grad, col_grad, sum_one / whole, sum_bias / whole, sum_two / whole)


def solution(mesh):
    in_specs = (P(None, "row", "col"), P("row", None), P("col", None), P(), P(), P())
    out_specs = (P("row", None), P("col", None), P(), P(), P())
    return jax.shard_map(shards, mesh=mesh, in_specs=in_specs, out_specs=out_specs, check_vma=False)
```

profile of v0, /device:TPU:1, one launch (start us, length us, event | category | flops | bytes accessed | tf_op | source)
XLA Modules:
  0.0 769.2 jit_solution(11806747635135335982)
XLA Ops:
  7.2 4.2 collective-permute-start.4
  11.4 1.3 collective-permute-start.5
  12.7 0.8 fusion.84
  13.5 5.7 collective-permute-start.6
  19.3 1.9 collective-permute-start.7
  21.2 5.1 collective-permute-start
  26.5 3.6 copy.67
  30.4 1.3 collective-permute-start.1
  31.7 0.8 convert_bitcast_fusion
  32.7 0.7 convert_bitcast_fusion.1
  33.4 2.7 select_convert_fusion
  36.1 2.3 copy.77
  39.3 5.9 broadcast_select_fusion
  45.2 2.7 copy.84
  47.9 2.6 slice.105
  50.5 6.2 copy.124
  56.7 3.2 select_convert_fusion.2
  63.5 2.3 select_convert_fusion.1
  66.5 3.8 add_divide_fusion
  70.3 3.5 copy.69
  73.8 3.6 copy.71
  77.4 1.2 pad_maximum_fusion.5
  78.7 4.8 collective-permute-start.2
  83.5 1.9 collective-permute-start.3
  85.4 0.7 pad_maximum_fusion.2
  86.2 5.2 collective-permute-done.3
  91.4 5.1 pad_maximum_fusion
  96.5 2.3 copy.73
  99.4 6.2 multiply_multiply_fusion
  105.5 2.7 copy.82
  108.3 2.5 slice.104
  110.8 6.1 copy.123
  116.9 3.8 convert_reduce_fusion
  124.1 86.2 %psum.38 = f32[64]{0:T(128)S(1)} all-reduce(f32[64]{0:T(128)S(1)} %get-tuple-element.14), channel_id=1, replica_groups=mesh['row'=32,'col'=8] {'row','col'}, use_global_device_ids=true, to_apply=%region_6.7 | all-reduce | flops 64 | bytes 512 | tf_op jit(solution)/shard_map/psum | solution.py:95
  210.7 0.9 copy.78
  211.6 2.2 fusion.17
  213.9 1.4 copy.80
  215.7 2.0 fusion.33
  217.7 0.7 copy.81
  219.0 1.4 fusion.36
  220.4 14.5 %psum.35 = f32[16,64]{1,0:T(8,128)S(1)} all-reduce(f32[16,64]{1,0:T(8,128)S(1)} %bitcast.166), channel_id=1, replica_groups=mesh['row'=32,'col'=8] {'col'}, use_global_device_ids=true, to_apply=%region_1.2 | all-reduce | flops 1024 | bytes 8192 | tf_op jit(solution)/shard_map/psum | solution.py:93
  235.5 0.7 pad_maximum_fusion.1
  236.3 250.7 %all-reduce.4.cloned.1.call-done = f32[256,64]{1,0:T(8,128)} async-done(((f32[256,64]{1,0:T(8,128)}), f32[256,64]{1,0:T(8,128)}) %all-reduce.4.cloned.1.call-update) | async-done | bytes 65552 | tf_op jit(solution)/shard_map/psum | solution.py:94
  487.0 0.9 broadcast_multiply_fusion.2
  487.9 0.7 copy.104
  488.6 270.1 %all-reduce.6.cloned.1.call-done = (f32[3,3,64,64]{3,2,1,0:T(8,128)}, f32[3,3,64,64]{3,2,1,0:T(8,128)}) async-done(((f32[3,3,64,64]{3,2,1,0:T(8,128)}, f32[3,3,64,64]{3,2,1,0:T(8,128)}), (f32[3,3,64,64]{3,2,1,0:T(8,128)}, f32[3,3,64,64]{3,2,1,0:T(8,128)})) %all-reduce.6.cloned.1.call-update) | async-done | bytes 294928 | tf_op jit(solution)/shard_map/psum | solution.py:95
  758.7 1.7 broadcast_multiply_fusion
  760.4 1.7 broadcast_multiply_fusion.1
  (85 shorter events, 11.6 us)
Async XLA Ops:
  7.2 92.2 %copy-start = (bf16[3,3,64,64]{3,2,1,0:T(8,128)(2,1)S(1)}, bf16[3,3,64,64]{3,2,1,0:T(8,128)(2,1)}, u32[]{:S(2)}) copy-start(bf16[3,3,64,64]{3,2,1,0:T(8,128)(2,1)} %param.11) | copy-start | bytes 221188
  7.2 479.8 %all-reduce.4.cloned.1.call-start = ((), (), s32[]{:S(2)}) async-start(), calls=%async_computation | async-start | bytes 262144 | tf_op jit(solution)/shard_map/psum | solution.py:94
  7.2 25.5 %collective-permute-start.4 = (bf16[16,64]{1,0:T(8,128)(2,1)}, bf16[16,64]{1,0:T(8,128)(2,1)S(1)}, u32[]{:S(2)}, u32[]{:S(2)}) collective-permute-start(bf16[16,64]{1,0:T(8,128)(2,1)} %param.7), channel_id=1, source_target_pairs={{0,8},{8,16},{16,24},{24,32},{32,40},{40,48},{48,56},{56,64},{64,7... | collective-permute-start | bytes 6152 | tf_op jit(solution)/shard_map/ppermute | solution.py:13
  11.4 21.3 %collective-permute-start.5 = (bf16[16,64]{1,0:T(8,128)(2,1)}, bf16[16,64]{1,0:T(8,128)(2,1)S(1)}, u32[]{:S(2)}, u32[]{:S(2)}) collective-permute-start(bf16[16,64]{1,0:T(8,128)(2,1)} %param.7), channel_id=1, source_target_pairs={{8,0},{16,8},{24,16},{32,24},{40,32},{48,40},{56,48},{64,56},{72,6... | collective-permute-start | bytes 6152 | tf_op jit(solution)/shard_map/ppermute | solution.py:16
  13.5 16.9 %collective-permute-start.6 = (bf16[16,64]{0,1:T(8,128)(2,1)S(1)}, bf16[16,64]{0,1:T(8,128)(2,1)S(1)}, u32[]{:S(2)}, u32[]{:S(2)}) collective-permute-start(bf16[16,64]{0,1:T(8,128)(2,1)S(1)} %get-tuple-element.22), channel_id=1, source_target_pairs={{0,1},{1,2},{2,3},{3,4},{4,5},{5,6},{6,7},{8,9},{9,10},{10,11},{11... | collective-permute-start | bytes 6152 | tf_op jit(solution)/shard_map/ppermute | solution.py:13
  19.3 12.5 %collective-permute-start.7 = (bf16[16,64]{0,1:T(8,128)(2,1)S(1)}, bf16[16,64]{0,1:T(8,128)(2,1)S(1)}, u32[]{:S(2)}, u32[]{:S(2)}) collective-permute-start(bf16[16,64]{0,1:T(8,128)(2,1)S(1)} %get-tuple-element.23), channel_id=1, source_target_pairs={{1,0},{2,1},{3,2},{4,3},{5,4},{6,5},{7,6},{9,8},{10,9},{11,10},{12... | collective-permute-start | bytes 6152 | tf_op jit(solution)/shard_map/ppermute | solution.py:16
  21.2 49.1 %collective-permute-start = (bf16[64,16,256]{2,1,0:T(8,128)(2,1)}, bf16[64,16,256]{2,1,0:T(8,128)(2,1)}, u32[]{:S(2)}, u32[]{:S(2)}) collective-permute-start(bf16[64,16,256]{2,1,0:T(8,128)(2,1)} %param.6), channel_id=1, source_target_pairs={{0,8},{8,16},{16,24},{24,32},{32,40},{40,48},{48,56},{56,64},{64,7... | collective-permute-start | bytes 1572872 | tf_op jit(solution)/shard_map/ppermute | solution.py:13
  30.4 43.4 %collective-permute-start.1 = (bf16[64,16,256]{2,1,0:T(8,128)(2,1)}, bf16[64,16,256]{2,1,0:T(8,128)(2,1)}, u32[]{:S(2)}, u32[]{:S(2)}) collective-permute-start(bf16[64,16,256]{2,1,0:T(8,128)(2,1)} %param.6), channel_id=1, source_target_pairs={{8,0},{16,8},{24,16},{32,24},{40,32},{48,40},{56,48},{64,56},{72,6... | collective-permute-start | bytes 1572872 | tf_op jit(solution)/shard_map/ppermute | solution.py:16
  38.4 0.9 copy-start.12
  38.4 0.9 copy-start.15
  45.2 2.8 copy-start.6
  50.5 6.2 copy-start.11
  56.7 3.2 copy-start.9
  77.4 8.0 %copy-start.10 = (f32[1,3,64,64]{3,2,1,0:T(8,128)S(1)}, f32[1,3,64,64]{3,2,1,0:T(8,128)}, u32[]{:S(2)}) copy-start(f32[1,3,64,64]{3,2,1,0:T(8,128)} %get-tuple-element.29) | copy-start | bytes 147460
  77.4 14.0 %copy-start.2 = (bf16[64,16,256]{0,1,2:T(8,128)(2,1)S(1)}, bf16[64,16,256]{0,1,2:T(8,128)(2,1)}, u32[]{:S(2)}) copy-start(bf16[64,16,256]{0,1,2:T(8,128)(2,1)} %copy.67) | copy-start | bytes 1572868
  77.4 14.0 %copy-start.4 = (bf16[64,16,256]{0,1,2:T(8,128)(2,1)S(1)}, bf16[64,16,256]{0,1,2:T(8,128)(2,1)}, u32[]{:S(2)}) copy-start(bf16[64,16,256]{0,1,2:T(8,128)(2,1)} %copy.69) | copy-start | bytes 1572868
  77.4 14.0 %copy-start.5 = (bf16[64,16,256]{0,1,2:T(8,128)(2,1)S(1)}, bf16[64,16,256]{0,1,2:T(8,128)(2,1)}, u32[]{:S(2)}) copy-start(bf16[64,16,256]{0,1,2:T(8,128)(2,1)} %copy.71) | copy-start | bytes 1572868
  78.7 7.5 collective-permute-start.2
  83.5 7.9 %collective-permute-start.3 = (bf16[64,48,16]{0,1,2:T(8,128)(2,1)S(1)}, bf16[64,48,16]{0,1,2:T(8,128)(2,1)S(1)}, u32[]{:S(2)}, u32[]{:S(2)}) collective-permute-start(bf16[64,48,16]{0,1,2:T(8,128)(2,1)S(1)} %get-tuple-element.21), channel_id=1, source_target_pairs={{1,0},{2,1},{3,2},{4,3},{5,4},{6,5},{7,6},{9,8},{10,9},{11,10},{12... | collective-permute-start | bytes 294920 | tf_op jit(solution)/shard_map/ppermute | solution.py:16
  91.4 7.9 %slice-start = ((s8[4718592]{0:T(1024)(128)(4,1)}), s8[4194304]{0:T(1024)(128)(4,1)S(1)}, s32[]{:S(2)}) async-start(s8[4718592]{0:T(1024)(128)(4,1)} %bitcast.163), calls=%async_computation.2 | async-start | bytes 8388608
  96.5 2.8 slice-start.1
  116.9 3.8 copy-start.7
  121.8 88.9 %copy-start.8 = (bf16[32,8,36,64]{3,1,2,0:T(8,128)(2,1)S(1)}, bf16[32,8,36,64]{3,1,2,0:T(8,128)(2,1)}, u32[]{:S(2)}) copy-start(bf16[32,8,36,64]{3,1,2,0:T(8,128)(2,1)} %get-tuple-element.24) | copy-start | bytes 3538948
  213.9 1.8 copy-start.13
  213.9 1.8 copy-start.14
  217.7 1.2 copy-start.3
  218.5 543.7 %copy-start.1 = (bf16[3,3,64,64]{3,2,1,0:T(8,128)(2,1)S(1)}, bf16[3,3,64,64]{3,2,1,0:T(8,128)(2,1)}, u32[]{:S(2)}) copy-start(bf16[3,3,64,64]{3,2,1,0:T(8,128)(2,1)} %param.11) | copy-start | bytes 221188
  220.4 538.3 %all-reduce.6.cloned.1.call-start = ((), (), s32[]{:S(2)}) async-start(), calls=%async_computation.1 | async-start | bytes 1179648 | tf_op jit(solution)/shard_map/psum | solution.py:95
Sparse Core Ops, SparseCore 0:
  220.5 266.4 all-reduce.3
  494.1 264.5 all-reduce.5
where the time goes:
time: 772 us; the launch traced here: 769 us
  waiting for transfers between devices  526 us (68%)
  blocking collectives  101 us (13%)
  local copies, waits for them, and re-layouts  45.4 us (6%)
  other arithmetic  35.1 us (5%)
  starting transfers between devices  26.3 us (3%)
  matrix products  20.9 us (3%)
  between operations  14.8 us (2%)
    psum x1, waiting for transfers between devices, shards(): lax.psum((grad_one, bias_part, grad_two), ('row', 'col'))  270 us
    psum x1, waiting for transfers between devices, shards(): col_grad = lax.psum(col_part, 'row') / math.sqrt(total_rows)  251 us
    psum x1, blocking collectives, shards(): lax.psum((grad_one, bias_part, grad_two), ('row', 'col'))  86.2 us
    ppermute x4, starting transfers between devices, extended(): lax.ppermute(lax.slice_in_dim(block, block.shape[dim] - width, None, axis...  19.8 us
    conv_general_dilated x11, local copies, waits for them, and re-layouts, conv_valid(): lax.conv_general_dilated(field[None], kernel, (1, 1), 'VALID', rhs_dilati...  18.6 us
    unnamed x40, local copies, waits for them, and re-layouts  17.6 us
  transfers between devices with their start and end apart: 10, of which 3 were waited for; matrix products, arithmetic and copies ran while one was open for 7% of the time, Pallas kernels for 0%

commit v1 on v0

--- a/solution.py
+++ b/solution.py
@@ -3,6 +3,7 @@
 import jax.numpy as jnp
 from jax import lax
 from jax.sharding import PartitionSpec as P
+from jax.lax import psum
 
 
 def extended(block, sides, width):
@@ -92,7 +93,8 @@
     bias_part = jnp.sum(inner_tile.astype(jnp.float32), axis=(1, 2))
     row_grad = lax.psum(row_part, "col") / math.sqrt(total_cols)
     col_grad = lax.psum(col_part, "row") / math.sqrt(total_rows)
-    sum_one, sum_bias, sum_two = lax.psum((grad_one, bias_part, grad_two), ("row", "col"))
+    panel_close = lambda content: psum(psum(content, "row"), "col")
+    sum_one, sum_bias, sum_two = panel_close((grad_one, bias_part, grad_two))
     whole = math.sqrt(total_rows * total_cols)
     return (row_grad, col_grad, sum_one / whole, sum_bias / whole, sum_two / whole)
 

time: 772 us -> 542 us (0.70)
  waiting for transfers between devices: 526 us -> 298 us
    psum x1, waiting for transfers between devices: 270 us -> 96.6 us  [shards(): panel_close = lambda content: psum(psum(content, 'row'), 'col')]
    psum x1, waiting for transfers between devices: 251 us -> 196 us  [shards(): col_grad = lax.psum(col_part, 'row') / math.sqrt(total_rows)]
    psum x1, blocking collectives: 86.2 us -> 71.9 us  [shards(): panel_close = lambda content: psum(psum(content, 'row'), 'col')]
    psum x1, blocking collectives: 14.5 us -> 26.7 us  [shards(): row_grad = lax.psum(row_part, 'col') / math.sqrt(total_cols)]
  transfers between devices with their start and end apart: 10 -> 10, of which waited for: 3 -> 3; matrix products, arithmetic and copies ran while one was open for 7% -> 9% of each run, Pallas kernels for 0% -> 0%
where the time goes in v1:
time: 542 us; the launch traced here: 539 us
  waiting for transfers between devices  298 us (55%)
  blocking collectives  98.6 us (18%)
  local copies, waits for them, and re-layouts  45.4 us (8%)
  other arithmetic  35.1 us (6%)
  starting transfers between devices  26.3 us (5%)
  matrix products  20.9 us (4%)
  between operations  14.8 us (3%)
    psum x1, waiting for transfers between devices, shards(): col_grad = lax.psum(col_part, 'row') / math.sqrt(total_rows)  196 us
    psum x1, waiting for transfers between devices, shards(): panel_close = lambda content: psum(psum(content, 'row'), 'col')  96.6 us
    psum x1, blocking collectives, shards(): panel_close = lambda content: psum(psum(content, 'row'), 'col')  71.9 us
    psum x1, blocking collectives, shards(): row_grad = lax.psum(row_part, 'col') / math.sqrt(total_cols)  26.7 us
    ppermute x4, starting transfers between devices, extended(): lax.ppermute(lax.slice_in_dim(block, block.shape[dim] - width, None, axis...  19.8 us
    conv_general_dilated x11, local copies, waits for them, and re-layouts, conv_valid(): lax.conv_general_dilated(field[None], kernel, (1, 1), 'VALID', rhs_dilati...  18.6 us
    unnamed x40, local copies, waits for them, and re-layouts  17.6 us
    conv_general_dilated x3, matrix products, conv_valid(): lax.conv_general_dilated(field[None], kernel, (1, 1), 'VALID', rhs_dilati...  14.1 us
  transfers between devices with their start and end apart: 10, of which 3 were waited for; matrix products, arithmetic and copies ran while one was open for 9% of the time, Pallas kernels for 0%

profile of v1, /device:TPU:1, one launch (start us, length us, event | category | flops | bytes accessed | tf_op | source)
XLA Modules:
  0.0 538.8 jit_solution(9954317080476350708)
XLA Ops:
  7.2 4.2 collective-permute-start.4
  11.4 1.3 collective-permute-start.5
  12.7 0.8 fusion.84
  13.5 5.7 %collective-permute-start.6 = (bf16[16,64]{0,1:T(8,128)(2,1)S(1)}, bf16[16,64]{0,1:T(8,128)(2,1)S(1)}, u32[]{:S(2)}, u32[]{:S(2)}) collective-permute-start(bf16[16,64]{0,1:T(8,128)(2,1)S(1)} %get-tuple-element.27), channel_id=1, source_target_pairs={{0,1},{1,2},{2,3},{3,4},{4,5},{5,6},{6,7},{8,9},{9,10},{10,11},{11... | collective-permute-start | bytes 6152 | tf_op jit(solution)/shard_map/ppermute | solution.py:14
  19.3 1.9 collective-permute-start.7
  21.2 5.1 collective-permute-start
  26.5 3.6 copy.67
  30.4 1.3 collective-permute-start.1
  31.7 0.8 convert_bitcast_fusion
  32.7 0.7 convert_bitcast_fusion.1
  33.4 2.7 select_convert_fusion
  36.1 2.3 copy.77
  39.3 5.9 %broadcast_select_fusion = f32[32,8,36,64]{3,1,2,0:T(8,128)S(1)} fusion(pred[8,36]{0,1:T(8,128)(4,1)S(1)} %copy-done.15, bf16[3,3,64,64]{3,2,1,0:T(8,128)(2,1)S(1)} %copy-done.12, bf16[64,48,1,7,16]{0,3,4,1,2:T(8,128)(2,1)S(1)} %slice.100, bf16[64,48,1,8,36]{0,3,4,1,2:T(8,128)(2,1)S(1)} %copy.77), kind=kOutput, calls=%fused_computation.34 | convolution fusion | flops 687734784 | bytes 4890912 | tf_op jit(solution)/shard_map/conv_general_dilated | solution.py:23
  45.2 2.7 copy.84
  47.9 2.6 slice.105
  50.5 6.2 %copy.124 = f32[32,1,272,64]{2,3,0,1:T(8,128)} copy(f32[32,1,272,64]{3,0,2,1:T(8,128)} %slice.105) | data formatting | bytes 4456448
  56.7 3.2 select_convert_fusion.2
  63.5 2.3 select_convert_fusion.1
  66.5 3.8 add_divide_fusion
  70.3 3.6 copy.69
  73.8 3.6 copy.71
  77.4 1.2 pad_maximum_fusion.5
  78.7 4.8 collective-permute-start.2
  83.5 1.9 collective-permute-start.3
  85.4 0.7 pad_maximum_fusion.2
  86.2 5.2 collective-permute-done.3
  91.4 5.1 pad_maximum_fusion
  96.5 2.3 copy.73
  99.3 6.2 %multiply_multiply_fusion = (bf16[32,8,36,64]{3,1,2,0:T(8,128)(2,1)}, f32[32,8,36,64]{3,1,2,0:T(8,128)S(1)}) fusion(f32[32,8,36,64]{3,1,2,0:T(8,128)S(1)} %bitcast.164, f32[64]{0:T(128)S(1)} %copy-done.11, bf16[3,3,64,64]{3,2,1,0:T(8,128)(2,1)S(1)} %copy-done, bf16[64,48,1,7,16]{0,3,4,1,2:T(8,128)(2,1)S(1)} %slice.99, ...), kind=kOutput, calls=%fused_computation.18 | convolution fusion | flops 693633024 | bytes 8430112 | tf_op jit(solution)/shard_map/conv_general_dilated | solution.py:23
  105.5 2.7 copy.82
  108.2 2.5 slice.104
  110.8 6.2 %copy.123 = f32[32,1,272,64]{2,3,0,1:T(8,128)} copy(f32[32,1,272,64]{3,0,2,1:T(8,128)} %slice.104) | data formatting | bytes 4456448
  116.9 3.8 convert_reduce_fusion
  124.0 0.9 copy.78
  125.0 2.2 fusion.17
  127.2 1.4 copy.80
  129.0 2.0 fusion.33
  131.1 0.7 copy.81
  132.3 1.4 fusion.36
  133.7 0.7 pad_maximum_fusion.1
  134.5 71.9 %psum.60 = f32[64]{0:T(128)S(1)} all-reduce(f32[64]{0:T(128)S(1)} %get-tuple-element.21), channel_id=1, replica_groups=mesh['row'=32,'col'=8] {'row'}, use_global_device_ids=true, to_apply=%region_7.8 | all-reduce | flops 64 | bytes 512 | tf_op jit(solution)/shard_map/psum | solution.py:96
  206.4 26.7 %all-reduce.1 = (f32[16,64]{1,0:T(8,128)S(1)}, f32[64]{0:T(128)S(1)}) all-reduce(f32[16,64]{1,0:T(8,128)S(1)} %bitcast.166, f32[64]{0:T(128)S(1)} %psum.60), channel_id=1, replica_groups=mesh['row'=32,'col'=8] {'col'}, use_global_device_ids=true, to_apply=%region_1.2 | all-reduce | flops 1088 | bytes 8704 | tf_op jit(solution)/shard_map/psum | solution.py:94
  233.8 195.8 %all-reduce.6.cloned.1.call-done = (f32[256,64]{1,0:T(8,128)}, f32[3,3,64,64]{3,2,1,0:T(8,128)}, f32[3,3,64,64]{3,2,1,0:T(8,128)}) async-done(((f32[256,64]{1,0:T(8,128)}, f32[3,3,64,64]{3,2,1,0:T(8,128)}, f32[3,3,64,64]{3,2,1,0:T(8,128)}), (f32[256,64]{1,0:T(8,128)}, f32[3,3,64,64]{3,2,1,0:T(8,128)}, f32[3,3,64,64]{3,2,1,0:T(8,128)})) %all-reduce.6.cloned.1.call-update) | async-done | bytes 360464 | tf_op jit(solution)/shard_map/psum | solution.py:95
  430.1 0.9 broadcast_multiply_fusion.2
  431.0 0.7 copy.104
  431.8 96.6 %all-reduce.8.cloned.1.call-done = (f32[3,3,64,64]{3,2,1,0:T(8,128)}, f32[3,3,64,64]{3,2,1,0:T(8,128)}) async-done(((f32[3,3,64,64]{3,2,1,0:T(8,128)}, f32[3,3,64,64]{3,2,1,0:T(8,128)}), (f32[3,3,64,64]{3,2,1,0:T(8,128)}, f32[3,3,64,64]{3,2,1,0:T(8,128)})) %all-reduce.8.cloned.1.call-update) | async-done | bytes 294928 | tf_op jit(solution)/shard_map/psum | solution.py:96
  528.3 1.7 broadcast_multiply_fusion
  530.0 1.7 broadcast_multiply_fusion.1
  (85 shorter events, 11.6 us)
Async XLA Ops:
  7.2 92.1 %copy-start = (bf16[3,3,64,64]{3,2,1,0:T(8,128)(2,1)S(1)}, bf16[3,3,64,64]{3,2,1,0:T(8,128)(2,1)}, u32[]{:S(2)}) copy-start(bf16[3,3,64,64]{3,2,1,0:T(8,128)(2,1)} %param.11) | copy-start | bytes 221188
  7.2 422.4 %all-reduce.6.cloned.1.call-start = ((), (), s32[]{:S(2)}) async-start(), calls=%async_computation | async-start | bytes 1441792 | tf_op jit(solution)/shard_map/psum | solution.py:95
  7.2 25.5 %collective-permute-start.4 = (bf16[16,64]{1,0:T(8,128)(2,1)}, bf16[16,64]{1,0:T(8,128)(2,1)S(1)}, u32[]{:S(2)}, u32[]{:S(2)}) collective-permute-start(bf16[16,64]{1,0:T(8,128)(2,1)} %param.7), channel_id=1, source_target_pairs={{0,8},{8,16},{16,24},{24,32},{32,40},{40,48},{48,56},{56,64},{64,7... | collective-permute-start | bytes 6152 | tf_op jit(solution)/shard_map/ppermute | solution.py:14
  11.4 21.3 %collective-permute-start.5 = (bf16[16,64]{1,0:T(8,128)(2,1)}, bf16[16,64]{1,0:T(8,128)(2,1)S(1)}, u32[]{:S(2)}, u32[]{:S(2)}) collective-permute-start(bf16[16,64]{1,0:T(8,128)(2,1)} %param.7), channel_id=1, source_target_pairs={{8,0},{16,8},{24,16},{32,24},{40,32},{48,40},{56,48},{64,56},{72,6... | collective-permute-start | bytes 6152 | tf_op jit(solution)/shard_map/ppermute | solution.py:17
  13.5 16.9 %collective-permute-start.6 = (bf16[16,64]{0,1:T(8,128)(2,1)S(1)}, bf16[16,64]{0,1:T(8,128)(2,1)S(1)}, u32[]{:S(2)}, u32[]{:S(2)}) collective-permute-start(bf16[16,64]{0,1:T(8,128)(2,1)S(1)} %get-tuple-element.27), channel_id=1, source_target_pairs={{0,1},{1,2},{2,3},{3,4},{4,5},{5,6},{6,7},{8,9},{9,10},{10,11},{11... | collective-permute-start | bytes 6152 | tf_op jit(solution)/shard_map/ppermute | solution.py:14
  19.3 12.5 %collective-permute-start.7 = (bf16[16,64]{0,1:T(8,128)(2,1)S(1)}, bf16[16,64]{0,1:T(8,128)(2,1)S(1)}, u32[]{:S(2)}, u32[]{:S(2)}) collective-permute-start(bf16[16,64]{0,1:T(8,128)(2,1)S(1)} %get-tuple-element.28), channel_id=1, source_target_pairs={{1,0},{2,1},{3,2},{4,3},{5,4},{6,5},{7,6},{9,8},{10,9},{11,10},{12... | collective-permute-start | bytes 6152 | tf_op jit(solution)/shard_map/ppermute | solution.py:17
  21.2 49.1 %collective-permute-start = (bf16[64,16,256]{2,1,0:T(8,128)(2,1)}, bf16[64,16,256]{2,1,0:T(8,128)(2,1)}, u32[]{:S(2)}, u32[]{:S(2)}) collective-permute-start(bf16[64,16,256]{2,1,0:T(8,128)(2,1)} %param.6), channel_id=1, source_target_pairs={{0,8},{8,16},{16,24},{24,32},{32,40},{40,48},{48,56},{56,64},{64,7... | collective-permute-start | bytes 1572872 | tf_op jit(solution)/shard_map/ppermute | solution.py:14
  30.4 43.4 %collective-permute-start.1 = (bf16[64,16,256]{2,1,0:T(8,128)(2,1)}, bf16[64,16,256]{2,1,0:T(8,128)(2,1)}, u32[]{:S(2)}, u32[]{:S(2)}) collective-permute-start(bf16[64,16,256]{2,1,0:T(8,128)(2,1)} %param.6), channel_id=1, source_target_pairs={{8,0},{16,8},{24,16},{32,24},{40,32},{48,40},{56,48},{64,56},{72,6... | collective-permute-start | bytes 1572872 | tf_op jit(solution)/shard_map/ppermute | solution.py:17
  38.4 0.9 copy-start.12
  38.4 0.9 copy-start.15
  45.2 2.8 copy-start.6
  50.5 6.2 %copy-start.11 = (f32[64]{0:T(128)S(1)}, f32[64]{0:T(128)}, u32[]{:S(2)}) copy-start(f32[64]{0:T(128)} %param.10) | copy-start | bytes 772
  56.7 3.2 copy-start.9
  77.4 8.0 %copy-start.10 = (f32[1,3,64,64]{3,2,1,0:T(8,128)S(1)}, f32[1,3,64,64]{3,2,1,0:T(8,128)}, u32[]{:S(2)}) copy-start(f32[1,3,64,64]{3,2,1,0:T(8,128)} %get-tuple-element.34) | copy-start | bytes 147460
  77.4 14.0 %copy-start.2 = (bf16[64,16,256]{0,1,2:T(8,128)(2,1)S(1)}, bf16[64,16,256]{0,1,2:T(8,128)(2,1)}, u32[]{:S(2)}) copy-start(bf16[64,16,256]{0,1,2:T(8,128)(2,1)} %copy.67) | copy-start | bytes 1572868
  77.4 14.0 %copy-start.4 = (bf16[64,16,256]{0,1,2:T(8,128)(2,1)S(1)}, bf16[64,16,256]{0,1,2:T(8,128)(2,1)}, u32[]{:S(2)}) copy-start(bf16[64,16,256]{0,1,2:T(8,128)(2,1)} %copy.69) | copy-start | bytes 1572868
  77.4 14.0 %copy-start.5 = (bf16[64,16,256]{0,1,2:T(8,128)(2,1)S(1)}, bf16[64,16,256]{0,1,2:T(8,128)(2,1)}, u32[]{:S(2)}) copy-start(bf16[64,16,256]{0,1,2:T(8,128)(2,1)} %copy.71) | copy-start | bytes 1572868
  78.7 7.5 %collective-permute-start.2 = (bf16[64,48,16]{0,1,2:T(8,128)(2,1)S(1)}, bf16[64,48,16]{0,1,2:T(8,128)(2,1)S(1)}, u32[]{:S(2)}, u32[]{:S(2)}) collective-permute-start(bf16[64,48,16]{0,1,2:T(8,128)(2,1)S(1)} %get-tuple-element.25), channel_id=1, source_target_pairs={{0,1},{1,2},{2,3},{3,4},{4,5},{5,6},{6,7},{8,9},{9,10},{10,11},{11... | collective-permute-start | bytes 294920 | tf_op jit(solution)/shard_map/ppermute | solution.py:14
  83.5 7.9 %collective-permute-start.3 = (bf16[64,48,16]{0,1,2:T(8,128)(2,1)S(1)}, bf16[64,48,16]{0,1,2:T(8,128)(2,1)S(1)}, u32[]{:S(2)}, u32[]{:S(2)}) collective-permute-start(bf16[64,48,16]{0,1,2:T(8,128)(2,1)S(1)} %get-tuple-element.26), channel_id=1, source_target_pairs={{1,0},{2,1},{3,2},{4,3},{5,4},{6,5},{7,6},{9,8},{10,9},{11,10},{12... | collective-permute-start | bytes 294920 | tf_op jit(solution)/shard_map/ppermute | solution.py:17
  91.4 7.9 %slice-start = ((s8[4718592]{0:T(1024)(128)(4,1)}), s8[4194304]{0:T(1024)(128)(4,1)S(1)}, s32[]{:S(2)}) async-start(s8[4718592]{0:T(1024)(128)(4,1)} %bitcast.163), calls=%async_computation.2 | async-start | bytes 8388608
  96.5 2.8 slice-start.1
  116.9 3.8 copy-start.7
  121.8 2.2 copy-start.8
  127.2 1.8 copy-start.13
  127.2 1.8 copy-start.14
  131.1 1.2 copy-start.3
  131.8 399.9 %copy-start.1 = (bf16[3,3,64,64]{3,2,1,0:T(8,128)(2,1)S(1)}, bf16[3,3,64,64]{3,2,1,0:T(8,128)(2,1)}, u32[]{:S(2)}) copy-start(bf16[3,3,64,64]{3,2,1,0:T(8,128)(2,1)} %param.11) | copy-start | bytes 221188
  134.5 393.8 %all-reduce.8.cloned.1.call-start = ((), (), s32[]{:S(2)}) async-start(), calls=%async_computation.1 | async-start | bytes 1179648 | tf_op jit(solution)/shard_map/psum | solution.py:96
Sparse Core Ops, SparseCore 0:
  134.6 294.9 all-reduce.5
  432.5 95.8 all-reduce.7
